TPU v7x, 32 devices: a whole 2x2x4 slice. The times are simulated.
32 devices in a mesh: lon: 8 (over y, x, core), head: 4 (over z).
Axes of the slice: x: 2, y: 2, z: 4, core: 2. Of those that a mesh axis runs over, the one named last changes fastest.
Arguments:
- latents: bfloat16 [3, 12, 64, 1024], P(None, 'head', 'lon'), may hold values from -16 to 16
- out_grad: bfloat16 [3, 12, 64, 1024], P(None, 'head', 'lon'), may hold values from -6 to 6
- qkv_weight: bfloat16 [16, 1024, 192], P('head'), as said below
- out_weight: bfloat16 [16, 64, 1024], replicated, may hold values from -0.1875 to 0.1875
Outputs:
- mixed: bfloat16 [3, 12, 64, 1024], P(None, 'head', 'lon')
- latent_grad: bfloat16 [3, 12, 64, 1024], P(None, 'head', 'lon')
- qkv_grad: float32 [16, 1024, 192], P('head')
Inputs may be any that keep to these rules, and one draw needn't show every extreme that they name: `qkv_weight`: entries lie within -14 / sqrt(1024) and 14 / sqrt(1024).
All inputs are finite; a program needn't handle non-finite values.
Results may differ from a plain program's by a relative error of at most 0.024.
The roundings to bfloat16 on the way count: a program that leaves them out, or rounds other values in their place, can miss the bound.
Values may be sent and summed in bfloat16 or wider, within the bound.
A program may use at most 64 MiB of HBM per device.

v0:
```python
import jax
import jax.numpy as jnp
from jax import lax
from jax.sharding import PartitionSpec as P

WIN_LAT = 6
WIN_LON = 8


MASKED = -1e30


def extended(block, sides, width):
    for axis, dim in sides:
        count = lax.axis_size(axis)
        forward = [(i, i + 1) for i in range(count - 1)]
        forward.append((count - 1, 0))
        backward = [(target, source) for source, target in forward]
        low = lax.ppermute(
            lax.slice_in_dim(block, block.shape[dim] - width, None, axis=dim), axis, forward
        )
        high = lax.ppermute(lax.slice_in_dim(block, 0, width, axis=dim), axis, backward)
        block = jnp.concatenate([low, block, high], axis=dim)
    return block


def shifted(block, axis, distance):
    devices = range(lax.axis_size(axis))
    route = [((i - distance) % len(devices), i) for i in devices]
    return lax.ppermute(block, axis, route)


def softmax_rows(query_rows, key_rows, valid, score_scale_factor):
    score_matrix = (
        jnp.einsum("fud,fwd->fuw", query_rows, key_rows, preferred_element_type=jnp.float32)
        * score_scale_factor
    )
    score_matrix = jnp.where(valid[:, None, :], score_matrix, MASKED)
    row_max = jnp.max(score_matrix, axis=-1, keepdims=True)
    powers = jnp.exp(score_matrix - row_max)
    return powers / jnp.sum(powers, axis=-1, keepdims=True)


def attend_block(pack, head_width, score_scale_factor):
    query_rows, key_value_pairs, valid = pack
    probs = softmax_rows(query_rows, key_value_pairs[..., :head_width], valid, score_scale_factor)
    probabilities_bfloat = probs.astype(jnp.bfloat16)
    attended_values = jnp.einsum(
        "ucf,ufg->ucg",
        probabilities_bfloat,
        key_value_pairs[..., head_width:],
        preferred_element_type=jnp.float32,
    )
    return attended_values.astype(jnp.bfloat16)


def attend_grad(pack, head_width, score_scale_factor):
    query_rows, key_value_pairs, valid, outer_gradient = pack
    key_portion = key_value_pairs[..., :head_width]
    value_portion = key_value_pairs[..., head_width:]
    probs = softmax_rows(query_rows, key_portion, valid, score_scale_factor)
    probabilities_bfloat = probs.astype(jnp.bfloat16)
    probability_gradient = jnp.einsum(
        "fud,fwd->fuw", outer_gradient, value_portion, preferred_element_type=jnp.float32
    )
    centre = jnp.sum(probs * probability_gradient, axis=-1, keepdims=True)
    score_gradient = (probs * (probability_gradient - centre)).astype(jnp.bfloat16)
    query_gradient = (
        jnp.einsum("ucf,ufg->ucg", score_gradient, key_portion, preferred_element_type=jnp.float32)
        * score_scale_factor
    )
    key_gradient = (
        jnp.einsum("txd,txr->tdr", score_gradient, query_rows, preferred_element_type=jnp.float32)
        * score_scale_factor
    )
    value_gradient = jnp.einsum(
        "txd,txr->tdr", probabilities_bfloat, outer_gradient, preferred_element_type=jnp.float32
    )
    return (query_gradient, jnp.concatenate([key_gradient, value_gradient], axis=-1))


def window_rows(values, windows):
    levels, lat_rows, columns, per_dev, inner = values.shape
    shaped = values.reshape(levels, windows, WIN_LAT, columns, per_dev, inner)
    return shaped.transpose(4, 1, 0, 2, 3, 5).reshape(
        per_dev * windows, levels * WIN_LAT * columns, inner
    )


def unwindow_rows(values, levels, windows, columns, per_dev):
    inner = values.shape[-1]
    shaped = values.reshape(per_dev, windows, levels, WIN_LAT, columns, inner).transpose(
        2, 1, 3, 4, 0, 5
    )
    return shaped.reshape(levels, windows * WIN_LAT, columns, per_dev, inner)


def window_keys(kv_ext, windows):
    levels, lat_rows, key_cols, per_dev, inner = kv_ext.shape
    half_lat = WIN_LAT // 2
    padded = jnp.pad(kv_ext, ((0, 0), (half_lat, half_lat), (0, 0), (0, 0), (0, 0)))
    lower = padded[:, :lat_rows].reshape(levels, windows, WIN_LAT, key_cols, per_dev, inner)
    upper = padded[:, WIN_LAT : lat_rows + WIN_LAT].reshape(
        levels, windows, WIN_LAT, key_cols, per_dev, inner
    )
    joined = jnp.concatenate([lower, upper], axis=2)
    return joined.transpose(4, 1, 0, 2, 3, 5).reshape(
        per_dev * windows, levels * 2 * WIN_LAT * key_cols, inner
    )


def unwindow_keys(grads, levels, windows, key_cols, per_dev):
    inner = grads.shape[-1]
    lat_rows = windows * WIN_LAT
    half_lat = WIN_LAT // 2
    shaped = grads.reshape(per_dev, windows, levels, 2 * WIN_LAT, key_cols, inner).transpose(
        2, 1, 3, 4, 0, 5
    )
    lower = shaped[:, :, :WIN_LAT].reshape(levels, lat_rows, key_cols, per_dev, inner)
    upper = shaped[:, :, WIN_LAT:].reshape(levels, lat_rows, key_cols, per_dev, inner)
    summed = jnp.pad(lower, ((0, 0), (0, WIN_LAT), (0, 0), (0, 0), (0, 0))) + jnp.pad(
        upper, ((0, 0), (WIN_LAT, 0), (0, 0), (0, 0), (0, 0))
    )
    return summed[:, half_lat : half_lat + lat_rows]


def key_valid(levels, windows, key_cols, per_dev, lat_rows):
    lat_index = (
        WIN_LAT * jnp.arange(windows)[:, None] - WIN_LAT // 2 + jnp.arange(2 * WIN_LAT)[None, :]
    )
    inside = (lat_index >= 0) & (lat_index < lat_rows)
    spread = jnp.broadcast_to(
        inside[None, :, None, :, None], (per_dev, windows, levels, 2 * WIN_LAT, key_cols)
    )
    return spread.reshape(per_dev * windows, -1)


def to_blocks(values):
    return values.reshape((values.shape[0] // 4, 4) + values.shape[1:])


def from_blocks(values):
    return values.reshape((-1,) + values.shape[2:])


def body(latents, out_grad, qkv_weight, out_weight):
    levels, lat_dev, columns, model_width = latents.shape
    groups = lax.axis_size("head")
    lat_rows = lat_dev * groups
    per_dev = qkv_weight.shape[0]
    head_count = out_weight.shape[0]
    head_width = out_weight.shape[1]
    score_scale_factor = head_width ** (-0.5)
    windows = lat_rows // WIN_LAT
    half_lon = WIN_LON // 2
    out_flat = out_weight.reshape(head_count * head_width, model_width)
    band_rows = lax.all_gather(latents, "head", axis=1, tiled=True)
    projected = jnp.einsum(
        "lawd,hdc->lawhc", band_rows, qkv_weight, preferred_element_type=jnp.float32
    ).astype(jnp.bfloat16)
    kv_ext = extended(projected[..., head_width:], (("lon", 2),), half_lon)
    key_cols = kv_ext.shape[2]
    query_rows = window_rows(projected[..., :head_width], windows)
    key_value_pairs = window_keys(kv_ext, windows)
    valid = key_valid(levels, windows, key_cols, per_dev, lat_rows)
    attended_values = lax.map(
        lambda pack: attend_block(pack, head_width, score_scale_factor),
        (to_blocks(query_rows), to_blocks(key_value_pairs), to_blocks(valid)),
    )
    attended_values = unwindow_rows(from_blocks(attended_values), levels, windows, columns, per_dev)
    attended_values = attended_values.reshape(levels, lat_rows, columns, per_dev * head_width)
    token_attended = lax.all_to_all(
        attended_values, "head", split_axis=1, concat_axis=3, tiled=True
    )
    mixed = jnp.dot(
        token_attended.reshape(-1, head_count * head_width),
        out_flat,
        preferred_element_type=jnp.float32,
    )
    mixed = mixed.astype(jnp.bfloat16).reshape(latents.shape)
    token_grad = jnp.dot(
        out_grad.reshape(-1, model_width), out_flat.T, preferred_element_type=jnp.float32
    ).astype(jnp.bfloat16)
    token_grad = token_grad.reshape(levels, lat_dev, columns, head_count * head_width)
    band_grad = lax.all_to_all(token_grad, "head", split_axis=3, concat_axis=1, tiled=True)
    band_grad = window_rows(
        band_grad.reshape(levels, lat_rows, columns, per_dev, head_width), windows
    )
    query_gradient, pair_grad = lax.map(
        lambda pack: attend_grad(pack, head_width, score_scale_factor),
        (to_blocks(query_rows), to_blocks(key_value_pairs), to_blocks(valid), to_blocks(band_grad)),
    )
    query_gradient = unwindow_rows(from_blocks(query_gradient), levels, windows, columns, per_dev)
    ext_grad = unwindow_keys(from_blocks(pair_grad), levels, windows, key_cols, per_dev)
    west_edge = ext_grad[:, :, half_lon + columns :].astype(jnp.bfloat16)
    east_edge = ext_grad[:, :, :half_lon].astype(jnp.bfloat16)
    from_west = shifted(west_edge, "lon", 1).astype(jnp.float32)
    from_east = shifted(east_edge, "lon", -1).astype(jnp.float32)
    own_grad = ext_grad[:, :, half_lon : half_lon + columns]
    own_grad = own_grad + jnp.pad(
        from_west, ((0, 0), (0, 0), (0, columns - half_lon), (0, 0), (0, 0))
    )
    own_grad = own_grad + jnp.pad(
        from_east, ((0, 0), (0, 0), (columns - half_lon, 0), (0, 0), (0, 0))
    )
    projected_grad = jnp.concatenate([query_gradient, own_grad], axis=-1).astype(jnp.bfloat16)
    grad_tokens = lax.all_to_all(
        projected_grad.reshape(levels, lat_rows, columns, per_dev * 3 * head_width),
        "head",
        split_axis=1,
        concat_axis=3,
        tiled=True,
    )
    grad_flat = grad_tokens.reshape(-1, head_count * 3 * head_width)
    piece = lax.all_gather(qkv_weight, "head", axis=0, tiled=True)
    part_cols = grad_flat
    part_cols = part_cols.reshape(grad_flat.shape[0], piece.shape[0], 3 * head_width)
    latent_sum = jnp.einsum("rnc,ndc->rd", part_cols, piece, preferred_element_type=jnp.float32)
    local_grad = jnp.einsum(
        "lawd,lawhc->hdc", band_rows, projected_grad, preferred_element_type=jnp.float32
    )
    latent_grad = latent_sum.astype(jnp.bfloat16).reshape(latents.shape)
    qkv_grad = lax.psum(local_grad.astype(jnp.bfloat16), "lon").astype(jnp.float32)
    return (mixed, latent_grad, qkv_grad)


def solution(mesh):
    placed = (
        P(None, "head", "lon", None),
        P(None, "head", "lon", None),
        P("head", None, None),
        P(),
    )
    return jax.shard_map(
        body,
        mesh=mesh,
        in_specs=placed,
        out_specs=(
            P(None, "head", "lon", None),
            P(None, "head", "lon", None),
            P("head", None, None),
        ),
        check_vma=False,
    )
```

profile of v0, /device:TPU:0, one launch (start us, length us, event | category | flops | bytes accessed | tf_op | source)
XLA Modules:
  0.0 256.5 jit_solution(5610650860525034494)
XLA Ops:
  8.0 18.5 %all_gather.6 = bf16[3,12,8,1024]{3,2,1,0:T(8,128)(2,1)S(1)} all-gather(bf16[3,3,8,1024]{3,2,1,0:T(8,128)(2,1)} %param.8), channel_id=1, replica_groups=mesh['lon'=8,'head'=4] {'head'}, dimensions={1}, use_global_device_ids=true | all-gather | bytes 737280 | tf_op jit(solution)/shard_map/all_gather | solution.py:157
  26.5 2.4 fusion.82
  29.0 1.0 fusion.110
  30.0 2.6 %collective-permute-start.1 = (bf16[3,12,4,4,128]{4,2,3,1,0:T(4,128)(2,1)}, bf16[3,12,4,4,128]{4,2,3,1,0:T(4,128)(2,1)}, u32[]{:S(2)}, u32[]{:S(2)}) collective-permute-start(bf16[3,12,4,4,128]{4,2,3,1,0:T(4,128)(2,1)} %get-tuple-element.142), channel_id=1, source_target_pairs={{4,0},{8,4},{12,8},{16,12},{20,16},{24,20},{28,24},{0,28},{5,1},{9... | collective-permute-start | bytes 442376 | tf_op jit(solution)/shard_map/ppermute | solution.py:22
  32.7 0.8 convolution_convert_fusion.1
  33.4 3.5 %copy.70 = bf16[3,3,8,1024]{2,1,0,3:T(4,128)(2,1)} copy(bf16[3,3,8,1024]{3,2,1,0:T(8,128)(2,1)S(1)} %bitcast.179) | data formatting | bytes 294912 | tf_op jit(solution)/shard_map/reshape | solution.py:184
  36.9 5.0 %reshape.107 = bf16[4,2,9216]{2,1,0:T(2,128)(2,1)} reshape(bf16[1024,3,3,8]{3,2,1,0:T(4,128)(2,1)} %bitcast.162) | data formatting | bytes 294912
  41.9 5.0 %all-to-all-start.1 = ((bf16[4,2,9216]{2,1,0:T(2,128)(2,1)}), bf16[4,2,9216]{2,1,0:T(2,128)(2,1)S(1)}, u32[]{:S(2)}, u32[]{:S(2)}) async-start(bf16[4,2,9216]{2,1,0:T(2,128)(2,1)} %reshape.107), calls=%async_computation.1 | async-start | bytes 294912 | tf_op jit(solution)/shard_map/all_to_all | solution.py:185
  47.2 0.9 copy.64
  48.2 0.7 reshape_reshape.35
  48.9 1.4 fusion.90
  50.7 1.3 copy.94
  52.0 1.7 copy.65
  53.7 3.9 %reshape.108 = bf16[1024,3,3,8]{3,2,1,0:T(4,128)(2,1)} reshape(bf16[4,2,9216]{2,1,0:T(2,128)(2,1)S(1)} %all-to-all-done.1) | data formatting | bytes 294912
  57.6 3.9 %copy.72 = bf16[3,4,3,8,256]{4,3,2,1,0:T(8,128)(2,1)S(1)} copy(bf16[3,4,3,8,256]{3,2,0,4,1:T(4,128)(2,1)} %bitcast.163) | data formatting | bytes 294912 | tf_op jit(solution)/shard_map/all_to_all | solution.py:185
  61.5 0.9 reshape_reshape.40
  62.4 1.7 copy.73
  64.1 1.9 copy.76
  65.9 28.6 %while.23 = (s32[]{:T(128)}, bf16[2,4,144,64]{2,3,1,0:T(8,128)(2,1)}, f32[2,4,576,128]{3,2,1,0:T(8,128)}, pred[2,4,576]{2,1,0:T(4,128)(4,1)}, bf16[2,4,144,64]{2...) while((s32[]{:T(128)}, ...), condition=%wide.region_8.9_spmd, body=%wide.region_4.8_spmd.sunk | while | flops 217128960 | bytes 45105476 | solution.py:189
  65.9 1.0 dynamic-slice_bitcast_fusion.11
  67.6 2.9 %fusion.151 = (f32[4,144]{1,0:T(4,128)S(1)}, f32[4,144,576]{2,1,0:T(8,128)}) fusion(pred[4,576]{1,0:T(4,128)(4,1)S(1)} %dynamic-slice_bitcast_fusion.10, bf16[4,576,128]{1,2,0:T(8,128)(2,1)} %dynamic-slice_bitcast_fusion.11, bf16[2,4,144,64]{2,3,1,0:T(8,128)(2,1)} %get-tuple-element.263, s32[]{:T(128)} %get-tuple-element.251), kind=kOutput, calls=%fused_computation.94.clone.1 | convolution fusion | flops 43795008 | bytes 1790976 | tf_op jit(solution)/shard_map/while/body/eval_jaxpr/sub | solution.py:40
  70.5 2.2 multiply_reduce_fusion.2
  73.9 0.8 copy-done.16
  75.2 1.4 copy.115
  76.6 2.5 constant_dynamic-update-slice_fusion.2
  79.2 1.1 fusion.152
  80.3 1.0 dynamic-slice_bitcast_fusion.11
  81.9 2.9 %fusion.151 = (f32[4,144]{1,0:T(4,128)S(1)}, f32[4,144,576]{2,1,0:T(8,128)}) fusion(pred[4,576]{1,0:T(4,128)(4,1)S(1)} %dynamic-slice_bitcast_fusion.10, bf16[4,576,128]{1,2,0:T(8,128)(2,1)} %dynamic-slice_bitcast_fusion.11, bf16[2,4,144,64]{2,3,1,0:T(8,128)(2,1)} %get-tuple-element.263, s32[]{:T(128)} %get-tuple-element.251), kind=kOutput, calls=%fused_computation.94.clone.1 | convolution fusion | flops 43795008 | bytes 1790976 | tf_op jit(solution)/shard_map/while/body/eval_jaxpr/sub | solution.py:40
  84.8 2.2 multiply_reduce_fusion.2
  88.2 0.8 copy-done.16
  89.5 1.4 copy.115
  90.9 2.5 constant_dynamic-update-slice_fusion.2
  93.5 1.1 fusion.152
  94.5 1.8 fusion.107
  96.5 0.7 copy.81
  97.4 0.7 copy.83
  98.8 0.7 copy-done.8
  99.5 0.9 fusion.108
  100.4 2.6 %collective-permute-start.3 = (bf16[3,12,4,4,128]{4,1,2,3,0:T(8,128)(2,1)}, bf16[3,12,4,4,128]{4,1,2,3,0:T(8,128)(2,1)}, u32[]{:S(2)}, u32[]{:S(2)}) collective-permute-start(bf16[3,12,4,4,128]{4,1,2,3,0:T(8,128)(2,1)} %get-tuple-element.138), channel_id=1, source_target_pairs={{4,0},{8,4},{12,8},{16,12},{20,16},{24,20},{28,24},{0,28},{5,1},{9... | collective-permute-start | bytes 442376 | tf_op jit(solution)/shard_map/ppermute | solution.py:30
  103.1 1.8 copy.77
  104.9 1.0 copy.78
  106.1 1.8 collective-permute-done.2
  107.9 1.7 fusion.93
  109.6 0.7 copy-done.12
  110.4 2.5 fusion.81
  113.6 11.2 %while.22 = (s32[]{:T(128)}, bf16[2,4,144,64]{2,3,1,0:T(8,128)(2,1)}, pred[2,4,576]{2,1,0:T(4,128)(4,1)S(1)}, bf16[2,4,144,64]{2,3,1,0:T(8,128)(2,1)}, bf16[2,4,576,128]{2,3,1,0:T(8,128)(2,1)S(1)}, /*index=5*/s32[]{:T(128)}) while((s32[]{:T(128)}, bf16[2,4,144,64]{2,3,1,0:T(8,128)(2,1)}, pred[2,4,576]{2,1,0:T(4,128)(4,1)S(1)}, ...), condition=%wide.region_3.4_spmd, body=%wide.region_0.3_spmd.sunk | while | flops 130426560 | bytes 2571341 | solution.py:166
  113.6 1.0 dynamic-slice_bitcast_fusion.9
  114.6 1.8 fusion.141
  116.4 2.7 %fusion.142 = bf16[2,4,144,64]{2,3,1,0:T(8,128)(2,1)} fusion(bf16[2,4,144,64]{2,3,1,0:T(8,128)(2,1)} %get-tuple-element.232, s32[]{:T(128)} %get-tuple-element.231, f32[4,144]{1,0:T(4,128)S(1)} %fusion.141, bf16[4,576,128]{1,2,0:T(8,128)(2,1)} %dynamic-slice_bitcast_fusion.9, pred[4,576]{1,0:T(4,128)(4,1)S(1)} %dynamic-slice_bitcast_fusion.8, ...), kind=kOutput, calls=%fused_computation.7.clone.1 | convolution fusion | flops 86631552 | bytes 923136 | tf_op jit(solution)/shard_map/while/body/eval_jaxpr/ucf,ufg->ucg/dot_general | solution.py:48
  119.2 1.0 dynamic-slice_bitcast_fusion.9
  120.1 1.8 fusion.141
  122.0 2.8 %fusion.142 = bf16[2,4,144,64]{2,3,1,0:T(8,128)(2,1)} fusion(bf16[2,4,144,64]{2,3,1,0:T(8,128)(2,1)} %get-tuple-element.232, s32[]{:T(128)} %get-tuple-element.231, f32[4,144]{1,0:T(4,128)S(1)} %fusion.141, bf16[4,576,128]{1,2,0:T(8,128)(2,1)} %dynamic-slice_bitcast_fusion.9, pred[4,576]{1,0:T(4,128)(4,1)S(1)} %dynamic-slice_bitcast_fusion.8, ...), kind=kOutput, calls=%fused_computation.7.clone.1 | convolution fusion | flops 86631552 | bytes 923136 | tf_op jit(solution)/shard_map/while/body/eval_jaxpr/ucf,ufg->ucg/dot_general | solution.py:48
  124.8 1.3 copy.66
  126.2 0.9 reshape.105
  127.1 5.1 %all-to-all-start = ((bf16[3,12,8,256]{3,2,0,1:T(8,128)(2,1)}), bf16[3,12,8,256]{3,2,0,1:T(8,128)(2,1)S(1)}, u32[]{:S(2)}, u32[]{:S(2)}) async-start(bf16[3,12,8,256]{3,2,0,1:T(8,128)(2,1)} %reshape.105), calls=%async_computation | async-start | bytes 294912 | tf_op jit(solution)/shard_map/all_to_all | solution.py:172
  133.0 1.3 reshape.106
  134.4 11.3 %all-to-all-done = bf16[3,12,8,256]{3,2,0,1:T(8,128)(2,1)S(1)} async-done(((bf16[3,12,8,256]{3,2,0,1:T(8,128)(2,1)}), bf16[3,12,8,256]{3,2,0,1:T(8,128)(2,1)S(1)}, u32[]{:S(2)}, u32[]{:S(2)}) %all-to-all-start) | async-done | bytes 147488 | tf_op jit(solution)/shard_map/all_to_all | solution.py:172
  145.7 3.5 %all-to-all-start.2 = ((bf16[3,12,8,768]{3,2,0,1:T(8,128)(2,1)}), bf16[3,12,8,768]{3,2,0,1:T(8,128)(2,1)S(1)}, u32[]{:S(2)}, u32[]{:S(2)}) async-start(bf16[3,12,8,768]{3,2,0,1:T(8,128)(2,1)} %reshape.106), calls=%async_computation.2 | async-start | bytes 884736 | tf_op jit(solution)/shard_map/all_to_all | solution.py:207
  149.2 1.1 convolution_convert_fusion.2
  150.4 21.6 %all-to-all-done.2 = bf16[3,12,8,768]{3,2,0,1:T(8,128)(2,1)S(1)} async-done(((bf16[3,12,8,768]{3,2,0,1:T(8,128)(2,1)}), bf16[3,12,8,768]{3,2,0,1:T(8,128)(2,1)S(1)}, u32[]{:S(2)}, u32[]{:S(2)}) %all-to-all-start.2) | async-done | bytes 442400 | tf_op jit(solution)/shard_map/all_to_all | solution.py:207
  172.7 0.8 all-reduce.7.cloned.1.call-done
  173.5 3.5 %convert_element_type.62 = f32[4,1024,192]{1,2,0:T(8,128)} convert(bf16[4,1024,192]{1,2,0:T(8,128)(2,1)} %all-reduce.7.cloned.1.call-done) | non-fusion elementwise | flops 786432 | bytes 4718592 | tf_op jit(solution)/shard_map/convert_element_type | solution.py:223
  177.0 67.2 %all-gather.2.cloned.1.call-done = bf16[16,1024,192]{1,2,0:T(8,128)(2,1)} async-done(((bf16[4,1024,192]{1,2,0:T(8,128)(2,1)}), bf16[16,1024,192]{1,2,0:T(8,128)(2,1)}) %all-gather.2.cloned.1.call-update) | async-done | bytes 6291472 | tf_op jit(solution)/shard_map/all_gather | solution.py:215
  244.2 4.8 %fusion.85 = bf16[72,1024]{1,0:T(8,128)(2,1)} fusion(bf16[16,1024,192]{1,2,0:T(8,128)(2,1)} %all-gather.2.cloned.1.call-done, bf16[72,16,192]{2,1,0:T(8,128)(2,1)S(1)} %reshape_reshape.44), kind=kOutput, calls=%fused_computation.76 | convolution fusion | flops 453058560 | bytes 6881280 | tf_op jit(solution)/shard_map/rnc,ndc->rd/dot_general | solution.py:218
  (94 shorter events, 9.0 us)
Async XLA Ops:
  8.0 24.7 %copy-start = (bf16[16,64,1024]{2,1,0:T(8,128)(2,1)S(1)}, bf16[16,64,1024]{2,1,0:T(8,128)(2,1)}, u32[]{:S(2)}) copy-start(bf16[16,64,1024]{2,1,0:T(8,128)(2,1)} %param.11) | copy-start | bytes 6291460
  26.5 2.4 copy-start.14
  26.5 6.1 %copy-start.18 = (bf16[3,3,8,1024]{3,2,1,0:T(8,128)(2,1)S(1)}, bf16[3,3,8,1024]{3,2,1,0:T(8,128)(2,1)}, u32[]{:S(2)}) copy-start(bf16[3,3,8,1024]{3,2,1,0:T(8,128)(2,1)} %param.9) | copy-start | bytes 442372
  30.0 18.9 %collective-permute-start = (bf16[3,12,4,4,128]{4,2,3,1,0:T(4,128)(2,1)}, bf16[3,12,4,4,128]{4,2,3,1,0:T(4,128)(2,1)}, u32[]{:S(2)}, u32[]{:S(2)}) collective-permute-start(bf16[3,12,4,4,128]{4,2,3,1,0:T(4,128)(2,1)} %get-tuple-element.141), channel_id=1, source_target_pairs={{0,4},{4,8},{8,12},{12,16},{16,20},{20,24},{24,28},{28,0},{1,5},{5... | collective-permute-start | bytes 442376 | tf_op jit(solution)/shard_map/ppermute | solution.py:19
  30.0 18.9 %collective-permute-start.1 = (bf16[3,12,4,4,128]{4,2,3,1,0:T(4,128)(2,1)}, bf16[3,12,4,4,128]{4,2,3,1,0:T(4,128)(2,1)}, u32[]{:S(2)}, u32[]{:S(2)}) collective-permute-start(bf16[3,12,4,4,128]{4,2,3,1,0:T(4,128)(2,1)} %get-tuple-element.142), channel_id=1, source_target_pairs={{4,0},{8,4},{12,8},{16,12},{20,16},{24,20},{28,24},{0,28},{5,1},{9... | collective-permute-start | bytes 442376 | tf_op jit(solution)/shard_map/ppermute | solution.py:22
  41.9 11.9 %all-to-all-start.1 = ((bf16[4,2,9216]{2,1,0:T(2,128)(2,1)}), bf16[4,2,9216]{2,1,0:T(2,128)(2,1)S(1)}, u32[]{:S(2)}, u32[]{:S(2)}) async-start(bf16[4,2,9216]{2,1,0:T(2,128)(2,1)} %reshape.107), calls=%async_computation.1 | async-start | bytes 294912 | tf_op jit(solution)/shard_map/all_to_all | solution.py:185
  46.8 126.6 %all-reduce.7.cloned.1.call-start = ((), (), s32[]{:S(2)}) async-start(), calls=%async_computation.4 | async-start | bytes 3145728 | tf_op jit(solution)/shard_map/psum | solution.py:223
  65.9 4.6 %copy-start.3 = (bf16[2,4,576,128]{2,3,1,0:T(8,128)(2,1)}, bf16[2,4,576,128]{2,3,1,0:T(8,128)(2,1)S(1)}, u32[]{:S(2)}) copy-start(bf16[2,4,576,128]{2,3,1,0:T(8,128)(2,1)S(1)} %get-tuple-element.264) | copy-start | bytes 3538948 | tf_op jit(solution)/shard_map/while
  70.5 2.2 copy-start.5
  72.7 1.0 copy-start.9
  73.6 1.5 copy-start.1
  73.6 1.1 copy-start.16
  76.6 2.5 copy-start.2
  76.6 2.5 copy-start.6
  76.6 3.6 %copy-start.4 = (bf16[2,4,576,128]{2,3,1,0:T(8,128)(2,1)S(1)}, bf16[2,4,576,128]{2,3,1,0:T(8,128)(2,1)}, u32[]{:S(2)}) copy-start(bf16[2,4,576,128]{2,3,1,0:T(8,128)(2,1)} %copy-done.3) | copy-start | bytes 3538948 | tf_op jit(solution)/shard_map/while
  80.3 4.6 %copy-start.3 = (bf16[2,4,576,128]{2,3,1,0:T(8,128)(2,1)}, bf16[2,4,576,128]{2,3,1,0:T(8,128)(2,1)S(1)}, u32[]{:S(2)}) copy-start(bf16[2,4,576,128]{2,3,1,0:T(8,128)(2,1)S(1)} %get-tuple-element.264) | copy-start | bytes 3538948 | tf_op jit(solution)/shard_map/while
  84.8 2.2 copy-start.5
  87.0 1.0 copy-start.9
  87.9 1.5 copy-start.1
  87.9 1.1 copy-start.16
  90.9 2.5 copy-start.2
  90.9 2.5 copy-start.6
  90.9 3.6 %copy-start.4 = (bf16[2,4,576,128]{2,3,1,0:T(8,128)(2,1)S(1)}, bf16[2,4,576,128]{2,3,1,0:T(8,128)(2,1)}, u32[]{:S(2)}) copy-start(bf16[2,4,576,128]{2,3,1,0:T(8,128)(2,1)} %copy-done.3) | copy-start | bytes 3538948 | tf_op jit(solution)/shard_map/while
  97.2 1.1 copy-start.7
  98.3 1.2 copy-start.8
  100.4 7.5 %collective-permute-start.2 = (bf16[3,12,4,4,128]{4,1,2,3,0:T(8,128)(2,1)}, bf16[3,12,4,4,128]{4,1,2,3,0:T(8,128)(2,1)}, u32[]{:S(2)}, u32[]{:S(2)}) collective-permute-start(bf16[3,12,4,4,128]{4,1,2,3,0:T(8,128)(2,1)} %get-tuple-element.137), channel_id=1, source_target_pairs={{28,0},{0,4},{4,8},{8,12},{12,16},{16,20},{20,24},{24,28},{29,1},{... | collective-permute-start | bytes 442376 | tf_op jit(solution)/shard_map/ppermute | solution.py:30
  100.4 7.5 %collective-permute-start.3 = (bf16[3,12,4,4,128]{4,1,2,3,0:T(8,128)(2,1)}, bf16[3,12,4,4,128]{4,1,2,3,0:T(8,128)(2,1)}, u32[]{:S(2)}, u32[]{:S(2)}) collective-permute-start(bf16[3,12,4,4,128]{4,1,2,3,0:T(8,128)(2,1)} %get-tuple-element.138), channel_id=1, source_target_pairs={{4,0},{8,4},{12,8},{16,12},{20,16},{24,20},{28,24},{0,28},{5,1},{9... | collective-permute-start | bytes 442376 | tf_op jit(solution)/shard_map/ppermute | solution.py:30
  106.1 3.6 %copy-start.10 = (bf16[3,12,8,4,64]{4,1,2,3,0:T(8,128)(2,1)}, bf16[3,12,8,4,64]{4,1,2,3,0:T(8,128)(2,1)S(1)}, u32[]{:S(2)}) copy-start(bf16[3,12,8,4,64]{4,1,2,3,0:T(8,128)(2,1)S(1)} %copy.84) | copy-start | bytes 442372
  106.1 4.3 %copy-start.15 = (bf16[3,12,8,1024]{3,2,1,0:T(8,128)(2,1)S(1)}, bf16[3,12,8,1024]{3,2,1,0:T(8,128)(2,1)}, u32[]{:S(2)}) copy-start(bf16[3,12,8,1024]{3,2,1,0:T(8,128)(2,1)} %copy-done.14) | copy-start | bytes 1769476
  109.6 0.8 copy-start.12
  112.9 0.7 copy-start.17
  113.0 131.2 %all-gather.2.cloned.1.call-start = ((), (), s32[]{:S(2)}) async-start(), calls=%async_computation.3 | async-start | bytes 7864320 | tf_op jit(solution)/shard_map/all_gather | solution.py:215
  124.8 7.4 %copy-start.11 = (bf16[3,12,8,4,64]{4,1,2,3,0:T(8,128)(2,1)S(1)}, bf16[3,12,8,4,64]{4,1,2,3,0:T(8,128)(2,1)}, u32[]{:S(2)}) copy-start(bf16[3,12,8,4,64]{4,1,2,3,0:T(8,128)(2,1)} %copy-done.10) | copy-start | bytes 442372
  124.8 7.4 %copy-start.13 = (bf16[3,12,8,4,128]{4,1,2,3,0:T(8,128)(2,1)S(1)}, bf16[3,12,8,4,128]{4,1,2,3,0:T(8,128)(2,1)}, u32[]{:S(2)}) copy-start(bf16[3,12,8,4,128]{4,1,2,3,0:T(8,128)(2,1)} %copy-done.12) | copy-start | bytes 884740
  127.1 18.6 %all-to-all-start = ((bf16[3,12,8,256]{3,2,0,1:T(8,128)(2,1)}), bf16[3,12,8,256]{3,2,0,1:T(8,128)(2,1)S(1)}, u32[]{:S(2)}, u32[]{:S(2)}) async-start(bf16[3,12,8,256]{3,2,0,1:T(8,128)(2,1)} %reshape.105), calls=%async_computation | async-start | bytes 294912 | tf_op jit(solution)/shard_map/all_to_all | solution.py:172
  145.7 26.3 %all-to-all-start.2 = ((bf16[3,12,8,768]{3,2,0,1:T(8,128)(2,1)}), bf16[3,12,8,768]{3,2,0,1:T(8,128)(2,1)S(1)}, u32[]{:S(2)}, u32[]{:S(2)}) async-start(bf16[3,12,8,768]{3,2,0,1:T(8,128)(2,1)} %reshape.106), calls=%async_computation.2 | async-start | bytes 884736 | tf_op jit(solution)/shard_map/all_to_all | solution.py:207
Sparse Core Ops, SparseCore 0:
  113.1 60.3 all-reduce.6
Sparse Core Ops, SparseCore 1:
  115.0 129.1 all-gather.1
where the time goes:
time: 258 us; the launch traced here: 256 us
  waiting for transfers between devices  103 us (40%)
  local copies, waits for them, and re-layouts  57.3 us (22%)
  matrix products  34.4 us (13%)
  starting transfers between devices  18.8 us (7%)
  blocking collectives  18.5 us (7%)
  between operations  15.8 us (6%)
  other arithmetic  8.26 us (3%)
    all_gather x1, waiting for transfers between devices, body(): piece = lax.all_gather(qkv_weight, 'head', axis=0, tiled=True)  67.2 us
    all_to_all x1, waiting for transfers between devices, body(): lax.all_to_all(projected_grad.reshape(levels, lat_rows, columns, per_dev...  21.6 us
    all_gather x1, blocking collectives, body(): band_rows = lax.all_gather(latents, 'head', axis=1, tiled=True)  18.5 us
    all_to_all x1, waiting for transfers between devices, body(): lax.all_to_all(attended_values, 'head', split_axis=1, concat_axis=3, tile...  11.3 us
    unnamed x25, local copies, waits for them, and re-layouts  10.7 us
    sub x4, matrix products, softmax_rows(): powers = jnp.exp(score_matrix - row_max)  9.4 us
    dynamic_update_slice x4, local copies, waits for them, and re-layouts, body(): lax.map(lambda pack: attend_grad(pack, head_width, score_scale_factor), (...  7.88 us
    dot_general x2, matrix products, attend_block(): jnp.einsum('ucf,ufg->ucg', probabilities_bfloat, key_value_pairs[..., hea...  5.53 us
  transfers between devices with their start and end apart: 9, of which 5 were waited for; matrix products, arithmetic and copies ran while one was open for 16% of the time, Pallas kernels for 0%

commit v1 on v0

v1 whole, which is shorter than its diff:
```python
import functools

import jax
import jax.numpy as jnp
import numpy as np
from jax import lax
from jax.experimental import pallas as pl
from jax.experimental.pallas import tpu as pltpu
from jax.sharding import PartitionSpec as P

WIN_LAT = 6
WIN_LON = 8
MASKED = -1e30
ROW_TILE = 16

F32 = jnp.float32
BF16 = jnp.bfloat16


def dot(a, b, dims=(1, 0)):
    return lax.dot_general(
        a, b, (((dims[0],), (dims[1],)), ((), ())), preferred_element_type=F32
    )


def remote(src, dst, sems, index, axis, device):
    send, recv = sems
    return pltpu.make_async_remote_copy(
        src_ref=src,
        dst_ref=dst,
        send_sem=send.at[index],
        recv_sem=recv.at[index],
        device_id={axis: device},
        device_id_type=pl.DeviceIdType.MESH,
    )


def kernel(
    dims,
    lat_ref,
    grad_ref,
    w_ref,
    out_w_ref,
    pick_ref,
    bias_ref,
    mixed_ref,
    latent_ref,
    qkv_ref,
    band,
    d_out,
    grad_send,
    query,
    keys,
    halo_send,
    acc,
    halo_grad_send,
    halo_grad,
    own_grad,
    attended,
    tokens,
    proj_grad,
    part,
    half_in,
    half_sum,
    chips_in,
    lat_send,
    lat_in,
    *sems,
):
    groups, count, heads, width, block, windows, edge = dims
    rows = groups * block
    win_rows = rows // windows
    scale = width ** (-0.5)
    gather_s, grad_s, att_s, lat_s, halo_s, hgrad_s, half_s, chip_s, all_s, pair_s = [
        (sems[2 * i], sems[2 * i + 1]) for i in range(10)
    ]
    me = lax.axis_index("lon")
    row = lax.axis_index("head")
    chips = count // 2
    core = lax.rem(me, 2)
    chip = lax.div(me, 2)
    pair = me + 1 - 2 * core
    east = lax.rem(me + 1, count)
    west = lax.rem(me + count - 1, count)
    pending = []

    def partner(d):
        return lax.rem(row + d, groups)

    def chip_at(d):
        return lax.rem(chip + d, chips)

    def block_of(g):
        return pl.ds(pl.multiple_of(g * block, ROW_TILE), block)

    offsets = sorted({1, count - 1} | set(range(2, count, 2)))
    barrier = pltpu.get_barrier_semaphore()
    for d in range(1, groups):
        pl.semaphore_signal(
            barrier, inc=1, device_id={"head": partner(d)}, device_id_type=pl.DeviceIdType.MESH
        )
    for d in offsets:
        pl.semaphore_signal(
            barrier,
            inc=1,
            device_id={"lon": lax.rem(me + d, count)},
            device_id_type=pl.DeviceIdType.MESH,
        )
    pl.semaphore_wait(barrier, groups - 1 + len(offsets))

    def launch(copy):
        copy.start()
        pending.append(copy)
        return copy

    mine = block_of(row)
    gathers = [
        launch(remote(lat_ref, band.at[mine], gather_s, d - 1, "head", partner(d)))
        for d in range(1, groups)
    ]
    band[mine, :] = lat_ref[...]

    cols = heads * width
    grads = []
    for d in range(1, groups + 1):
        g = partner(d)
        some = dot(
            grad_ref[...], out_w_ref[pl.ds(pl.multiple_of(g * cols, ROW_TILE), cols), :], (1, 1)
        ).astype(BF16)
        if d < groups:
            grad_send[d - 1] = some
            grads.append(
                launch(remote(grad_send.at[d - 1], d_out.at[mine], grad_s, d - 1, "head", g))
            )
        else:
            d_out[mine, :] = some
    for copy in gathers:
        copy.wait_recv()

    halos = []
    for h in range(heads):
        projected = dot(band[...], w_ref[h]).astype(BF16)
        query[h] = projected[:, :width]
        pairs = projected[:, width:]
        keys[h, 0:rows, :] = pairs
        copies = []
        for side, device in ((0, east), (1, west)):
            halo_send[side, h] = dot(pick_ref[side], pairs).astype(BF16)
            copies.append(
                launch(
                    remote(
                        halo_send.at[side, h],
                        keys.at[h, pl.ds(rows + side * edge, edge)],
                        halo_s,
                        (side, h),
                        "lon",
                        device,
                    )
                )
            )
        halos.append(copies)
    for copy in grads:
        copy.wait_recv()

    returns = []
    for h in range(heads):
        for copy in halos[h]:
            copy.wait_recv()
        acc[...] = jnp.zeros_like(acc)

        def window(w, carry):
            here = pl.ds(pl.multiple_of(w * win_rows, ROW_TILE), win_rows)
            q = query[h, here, :]
            k = keys[h, :, 0:width]
            v = keys[h, :, width : 2 * width]
            scores = dot(q, k, (1, 1)) * scale + bias_ref[w]
            powers = jnp.exp(scores - jnp.max(scores, axis=-1, keepdims=True))
            probs = powers / jnp.sum(powers, axis=-1, keepdims=True)
            probs_b = probs.astype(BF16)
            attended[here, h * width : (h + 1) * width] = dot(probs_b, v).astype(BF16)
            outer = d_out[here, h * width : (h + 1) * width]
            prob_grad = dot(outer, v, (1, 1))
            centre = jnp.sum(probs * prob_grad, axis=-1, keepdims=True)
            score_grad = (probs * (prob_grad - centre)).astype(BF16)
            proj_grad[here, 3 * h * width : (3 * h + 1) * width] = (
                dot(score_grad, k) * scale
            ).astype(BF16)
            acc[:, 0:width] += dot(score_grad, q, (0, 0)) * scale
            acc[:, width : 2 * width] += dot(probs_b, outer, (0, 0))
            return carry

        lax.fori_loop(0, windows, window, 0)
        own_grad[h] = acc[0:rows, :]
        copies = []
        for side, device in ((0, west), (1, east)):
            halo_grad_send[side, h] = acc[
                rows + side * edge : rows + (side + 1) * edge, :
            ].astype(BF16)
            copies.append(
                launch(
                    remote(
                        halo_grad_send.at[side, h],
                        halo_grad.at[side, h],
                        hgrad_s,
                        (side, h),
                        "lon",
                        device,
                    )
                )
            )
        returns.append(copies)

    sent = []
    for d in range(1, groups):
        sent.append(
            launch(
                remote(
                    attended.at[block_of(partner(d))],
                    tokens.at[row],
                    att_s,
                    d - 1,
                    "head",
                    partner(d),
                )
            )
        )
    tokens[row] = attended[mine, :]

    for h in range(heads):
        for copy in returns[h]:
            copy.wait_recv()
        total = own_grad[h]
        for side in range(2):
            total += dot(pick_ref[side], halo_grad[side, h], (0, 0))
        proj_grad[:, (3 * h + 1) * width : 3 * (h + 1) * width] = total.astype(BF16)

    depth = band.shape[1]
    half = depth // 2
    step = min(half, 256)

    def qkv_half(which):
        def one(i, carry):
            at = pl.multiple_of(which * half + i * step, 128)
            part[pl.ds(at, step), :] = dot(
                band[:, pl.ds(at, step)], proj_grad[...], (0, 0)
            ).astype(BF16)
            return carry

        lax.fori_loop(0, half // step, one, 0)

    qkv_half(1 - core)
    theirs = pl.ds(pl.multiple_of((1 - core) * half, ROW_TILE), half)
    ours = pl.ds(pl.multiple_of(core * half, ROW_TILE), half)
    halves = launch(remote(part.at[theirs], half_in, half_s, 0, "lon", pair))
    qkv_half(core)

    wide = min(depth, 256)

    def latent(i, carry):
        at = pl.ds(pl.multiple_of(i * wide, 128), wide)
        total = jnp.zeros((rows, wide), F32)
        for h in range(heads):
            total += dot(
                proj_grad[:, 3 * h * width : 3 * (h + 1) * width], w_ref[h, at, :], (1, 1)
            )
        lat_send[:, at] = total.astype(BF16)
        return carry

    lax.fori_loop(0, depth // wide, latent, 0)
    lats = [
        launch(
            remote(
                lat_send.at[block_of(partner(d))], lat_in.at[d - 1], lat_s, d - 1, "head", partner(d)
            )
        )
        for d in range(1, groups)
    ]

    halves.wait_recv()
    piece = half // chips
    half_sum[...] = (part[ours, :].astype(F32) + half_in[...].astype(F32)).astype(BF16)

    def piece_of(t):
        return pl.ds(pl.multiple_of(t * piece, ROW_TILE), piece)

    exchanged = [
        launch(
            remote(
                half_sum.at[piece_of(chip_at(d))],
                chips_in.at[d - 1],
                chip_s,
                d - 1,
                "lon",
                2 * chip_at(d) + core,
            )
        )
        for d in range(1, chips)
    ]

    for copy in sent:
        copy.wait_recv()
    mixed = jnp.zeros((block, depth), F32)
    for g in range(groups):
        mixed += dot(tokens[g], out_w_ref[g * cols : (g + 1) * cols, :])
    mixed_ref[...] = mixed.astype(BF16)

    for copy in exchanged:
        copy.wait_recv()
    total = half_sum[piece_of(chip), :].astype(F32)
    for d in range(1, chips):
        total += chips_in[d - 1].astype(F32)

    def result_of(t):
        return pl.ds(pl.multiple_of(core * half + t * piece, ROW_TILE), piece)

    final = result_of(chip)
    qkv_ref[final, :] = total.astype(BF16)
    spread = [
        launch(
            remote(
                qkv_ref.at[final], qkv_ref.at[final], all_s, d - 1, "lon", 2 * chip_at(d) + core
            )
        )
        for d in range(1, chips)
    ]
    shared = [launch(remote(qkv_ref.at[final], qkv_ref.at[final], pair_s, 0, "lon", pair))]

    for copy in lats:
        copy.wait_recv()
    total = lat_send[mine, :].astype(F32)
    for d in range(1, groups):
        total += lat_in[d - 1].astype(F32)
    latent_ref[...] = total.astype(BF16)

    for d in range(1, chips):
        spread[d - 1].wait_recv()
        came = result_of(lax.rem(chip + chips - d, chips))
        shared.append(launch(remote(qkv_ref.at[came], qkv_ref.at[came], pair_s, d, "lon", pair)))
    for copy in shared:
        copy.wait_recv()
    for copy in pending:
        copy.wait_send()


def tables(levels, lat_dev, groups, columns, windows, block):
    half = columns // 2
    lat_rows = lat_dev * groups
    edge = lat_rows * levels * half
    pick = np.zeros((2, edge, groups * block), np.float32)
    key_lat = np.full((groups * block,), -(10**6))
    for g in range(groups):
        for r in range(lat_dev):
            for level in range(levels):
                base = g * block + (r * levels + level) * columns
                key_lat[base : base + columns] = g * lat_dev + r
                at = ((g * lat_dev + r) * levels + level) * half
                for c in range(half):
                    pick[0, at + c, base + columns - half + c] = 1
                    pick[1, at + c, base + c] = 1
    edge_lat = np.repeat(np.arange(lat_rows), levels * half)
    lat = np.concatenate([key_lat, edge_lat, edge_lat])
    low = WIN_LAT * np.arange(windows)[:, None] - WIN_LAT // 2
    inside = (lat[None] >= low) & (lat[None] < low + 2 * WIN_LAT)
    bias = np.where(inside & (lat[None] >= 0), 0.0, MASKED).astype(np.float32)
    return pick, bias[:, None, :], edge


def body(latents, out_grad, qkv_weight, out_weight):
    levels, lat_dev, columns, model_width = latents.shape
    groups = lax.axis_size("head")
    count = lax.axis_size("lon")
    heads = qkv_weight.shape[0]
    width = out_weight.shape[1]
    windows = lat_dev * groups // WIN_LAT
    valid = levels * lat_dev * columns
    block = -(-valid // ROW_TILE) * ROW_TILE
    rows = groups * block
    pick, bias, edge = tables(levels, lat_dev, groups, columns, windows, block)
    keys = rows + 2 * edge
    cols = heads * width
    chips = count // 2
    half = model_width // 2

    def packed(x):
        x = x.transpose(1, 0, 2, 3).reshape(valid, model_width)
        return jnp.pad(x, ((0, block - valid), (0, 0)))

    def unpacked(x):
        return x[:valid].reshape(lat_dev, levels, columns, model_width).transpose(1, 0, 2, 3)

    dma = pltpu.SemaphoreType.DMA
    shapes = [
        (groups - 1,),
        (groups - 1,),
        (groups - 1,),
        (groups - 1,),
        (2, heads),
        (2, heads),
        (1,),
        (chips - 1,),
        (chips - 1,),
        (chips,),
    ]
    vmem = pl.BlockSpec(memory_space=pltpu.VMEM)
    mixed, latent_grad, qkv = pl.pallas_call(
        functools.partial(kernel, (groups, count, heads, width, block, windows, edge)),
        out_shape=(
            jax.ShapeDtypeStruct((block, model_width), BF16),
            jax.ShapeDtypeStruct((block, model_width), BF16),
            jax.ShapeDtypeStruct((model_width, 3 * cols), BF16),
        ),
        in_specs=[vmem] * 6,
        out_specs=(vmem,) * 3,
        scratch_shapes=[
            pltpu.VMEM((rows, model_width), BF16),
            pltpu.VMEM((rows, cols), BF16),
            pltpu.VMEM((groups - 1, block, cols), BF16),
            pltpu.VMEM((heads, rows, width), BF16),
            pltpu.VMEM((heads, keys, 2 * width), BF16),
            pltpu.VMEM((2, heads, edge, 2 * width), BF16),
            pltpu.VMEM((keys, 2 * width), F32),
            pltpu.VMEM((2, heads, edge, 2 * width), BF16),
            pltpu.VMEM((2, heads, edge, 2 * width), BF16),
            pltpu.VMEM((heads, rows, 2 * width), F32),
            pltpu.VMEM((rows, cols), BF16),
            pltpu.VMEM((groups, block, cols), BF16),
            pltpu.VMEM((rows, 3 * cols), BF16),
            pltpu.VMEM((model_width, 3 * cols), BF16),
            pltpu.VMEM((half, 3 * cols), BF16),
            pltpu.VMEM((half, 3 * cols), BF16),
            pltpu.VMEM((chips - 1, half // chips, 3 * cols), BF16),
            pltpu.VMEM((rows, model_width), BF16),
            pltpu.VMEM((groups - 1, block, model_width), BF16),
        ]
        + [dma(s) for s in shapes for _ in range(2)],
        compiler_params=pltpu.CompilerParams(
            collective_id=0, has_side_effects=True, vmem_limit_bytes=56 * 1024 * 1024
        ),
    )(
        packed(latents),
        packed(out_grad),
        qkv_weight,
        out_weight.reshape(-1, model_width),
        jnp.asarray(pick, BF16),
        jnp.asarray(bias),
    )
    qkv_grad = qkv.reshape(model_width, heads, 3 * width).transpose(1, 0, 2).astype(F32)
    return unpacked(mixed), unpacked(latent_grad), qkv_grad


def solution(mesh):
    placed = (
        P(None, "head", "lon", None),
        P(None, "head", "lon", None),
        P("head", None, None),
        P(),
    )
    return jax.shard_map(
        body,
        mesh=mesh,
        in_specs=placed,
        out_specs=(
            P(None, "head", "lon", None),
            P(None, "head", "lon", None),
            P("head", None, None),
        ),
        check_vma=False,
    )
```

time: 258 us -> 82.8 us (0.32)
  the two profiles are of different devices: /device:TPU:0 before, /device:TPU:9 now
where the time goes in v1:
time: 82.8 us; the launch traced here: 82.5 us
  Pallas kernels  69.3 us (84%)
  local copies, waits for them, and re-layouts  12.5 us (15%)
    pallas_call x1, Pallas kernels, body(): pl.pallas_call(functools.partial(kernel, (groups, count, heads, width, bl...  69.3 us
    unnamed x1, local copies, waits for them, and re-layouts  3.72 us
    convert_element_type x1, local copies, waits for them, and re-layouts, body(): qkv.reshape(model_width, heads, 3 * width).transpose(1, 0, 2).astype(F32)  3.07 us
    slice x2, local copies, waits for them, and re-layouts, unpacked(): x[:valid].reshape(lat_dev, levels, columns, model_width)  1.84 us
    transpose x2, local copies, waits for them, and re-layouts, packed(): x = x.transpose(1, 0, 2, 3).reshape(valid, model_width)  1.84 us

profile of v1, /device:TPU:9, one launch (start us, length us, event | category | flops | bytes accessed | tf_op | source)
XLA Modules:
  0.0 82.5 jit_solution(4454020517160433882)
XLA Ops:
  0.6 0.9 %copy.15 = bf16[3,3,8,1024]{3,2,1,0:T(8,128)(2,1)S(1)} copy(bf16[3,3,8,1024]{3,2,0,1:T(8,128)(2,1)} %bitcast.20) | data formatting | bytes 294912 | tf_op jit(solution)/shard_map/transpose | solution.py:385
  1.6 0.7 pad.7.lat_ref
  2.2 0.9 %copy.16 = bf16[3,3,8,1024]{3,2,1,0:T(8,128)(2,1)S(1)} copy(bf16[3,3,8,1024]{3,2,0,1:T(8,128)(2,1)} %bitcast.21) | data formatting | bytes 294912 | tf_op jit(solution)/shard_map/transpose | solution.py:385
  3.1 0.7 pad.8.grad_ref
  3.8 3.7 %copy.17.w_ref = bf16[4,1024,192]{2,1,0:T(8,128)(2,1)} copy(bf16[4,1024,192]{1,2,0:T(8,128)(2,1)} %param.8) | data formatting | bytes 3145728 | tf_op args[2]
  7.5 69.3 %shard_map.85 = (bf16[80,1024]{1,0:T(8,128)(2,1)}, bf16[80,1024]{1,0:T(8,128)(2,1)}, bf16[1024,768]{1,0:T(8,128)(2,1)}) custom-call(bf16[80,1024]{1,0:T(8,128)(2,1)} %pad.7.lat_ref, bf16[80,1024]{1,0:T(8,128)(2,1)} %pad.8.grad_ref, bf16[4,1024,192]{2,1,0:T(8,128)(2,1)} %copy.17.w_ref, bf16[1024,1024]{1,0:T(8,128)(2,1)} %bitcast.15, ...), custom_call_target="tpu_custom_call" | custom-call | tf_op jit(solution)/shard_map/pallas_call | solution.py:405
  76.9 0.9 %slice.6 = bf16[72,1024]{1,0:T(8,128)(2,1)S(1)} slice(bf16[80,1024]{1,0:T(8,128)(2,1)} %get-tuple-element.6), slice={[0:72], [0:1024]} | slice | bytes 294912 | tf_op jit(solution)/shard_map/slice | solution.py:389
  77.8 0.9 %slice.7 = bf16[72,1024]{1,0:T(8,128)(2,1)S(1)} slice(bf16[80,1024]{1,0:T(8,128)(2,1)} %get-tuple-element.7), slice={[0:72], [0:1024]} | slice | bytes 294912 | tf_op jit(solution)/shard_map/slice | solution.py:389
  78.7 0.7 copy_bitcast_fusion
  79.5 3.1 %copy.20 = f32[1024,768]{0,1:T(8,128)} copy(bf16[1024,768]{1,0:T(8,128)(2,1)} %get-tuple-element.8) | data formatting | bytes 4718592 | tf_op jit(solution)/shard_map/convert_element_type | solution.py:447

commit v2 on v1

--- a/solution.py
+++ b/solution.py
@@ -52,7 +52,8 @@
     query,
     keys,
     halo_send,
-    acc,
+    soft,
+    hard,
     halo_grad_send,
     halo_grad,
     own_grad,
@@ -68,6 +69,8 @@
     *sems,
 ):
     groups, count, heads, width, block, windows, edge = dims
+    levels, lat_dev, columns, depth = lat_ref.shape
+    cols = heads * width
     rows = groups * block
     win_rows = rows // windows
     scale = width ** (-0.5)
@@ -93,6 +96,19 @@
     def block_of(g):
         return pl.ds(pl.multiple_of(g * block, ROW_TILE), block)
 
+    mine = block_of(row)
+    def packed(ref):
+        parts = [ref[level, r].astype(F32) for r in range(lat_dev) for level in range(levels)]
+        if block > len(parts) * columns:
+            parts.append(jnp.zeros((block - len(parts) * columns, depth), F32))
+        return jnp.concatenate(parts, axis=0).astype(BF16)
+
+    def unpacked(ref, value):
+        for r in range(lat_dev):
+            for level in range(levels):
+                at = (r * levels + level) * columns
+                ref[level, r] = value[at : at + columns].astype(BF16)
+
     offsets = sorted({1, count - 1} | set(range(2, count, 2)))
     barrier = pltpu.get_barrier_semaphore()
     for d in range(1, groups):
@@ -106,6 +122,7 @@
             device_id={"lon": lax.rem(me + d, count)},
             device_id_type=pl.DeviceIdType.MESH,
         )
+    band[mine, :] = packed(lat_ref)
     pl.semaphore_wait(barrier, groups - 1 + len(offsets))
 
     def launch(copy):
@@ -113,19 +130,16 @@
         pending.append(copy)
         return copy
 
-    mine = block_of(row)
     gathers = [
-        launch(remote(lat_ref, band.at[mine], gather_s, d - 1, "head", partner(d)))
+        launch(remote(band.at[mine], band.at[mine], gather_s, d - 1, "head", partner(d)))
         for d in range(1, groups)
     ]
-    band[mine, :] = lat_ref[...]
-
-    cols = heads * width
+    out_grad = packed(grad_ref)
     grads = []
     for d in range(1, groups + 1):
         g = partner(d)
         some = dot(
-            grad_ref[...], out_w_ref[pl.ds(pl.multiple_of(g * cols, ROW_TILE), cols), :], (1, 1)
+            out_grad, out_w_ref[pl.ds(pl.multiple_of(g * cols, ROW_TILE), cols), :], (1, 1)
         ).astype(BF16)
         if d < groups:
             grad_send[d - 1] = some
@@ -138,10 +152,11 @@
         copy.wait_recv()
 
     halos = []
+    projected = dot(band[...], w_ref[...], (1, 1)).astype(BF16)
     for h in range(heads):
-        projected = dot(band[...], w_ref[h]).astype(BF16)
-        query[h] = projected[:, :width]
-        pairs = projected[:, width:]
+        base = 3 * h * width
+        query[h] = (projected[:, base : base + width].astype(F32) * scale).astype(BF16)
+        pairs = projected[:, base + width : base + 3 * width]
         keys[h, 0:rows, :] = pairs
         copies = []
         for side, device in ((0, east), (1, west)):
@@ -162,53 +177,67 @@
     for copy in grads:
         copy.wait_recv()
 
-    returns = []
-    for h in range(heads):
-        for copy in halos[h]:
+    for copies in halos:
+        for copy in copies:
             copy.wait_recv()
-        acc[...] = jnp.zeros_like(acc)
-
-        def window(w, carry):
-            here = pl.ds(pl.multiple_of(w * win_rows, ROW_TILE), win_rows)
-            q = query[h, here, :]
+
+    def window(some, w):
+        here = pl.ds(pl.multiple_of(w * win_rows, ROW_TILE), win_rows)
+        for h in some:
+            lanes = slice(h * width, (h + 1) * width)
             k = keys[h, :, 0:width]
             v = keys[h, :, width : 2 * width]
-            scores = dot(q, k, (1, 1)) * scale + bias_ref[w]
+            scores = dot(query[h, here, :], k, (1, 1)) + bias_ref[w]
+            prob_grad = dot(d_out[here, lanes], v, (1, 1))
             powers = jnp.exp(scores - jnp.max(scores, axis=-1, keepdims=True))
-            probs = powers / jnp.sum(powers, axis=-1, keepdims=True)
+            probs = powers * (1.0 / jnp.sum(powers, axis=-1, keepdims=True))
             probs_b = probs.astype(BF16)
-            attended[here, h * width : (h + 1) * width] = dot(probs_b, v).astype(BF16)
-            outer = d_out[here, h * width : (h + 1) * width]
-            prob_grad = dot(outer, v, (1, 1))
+            hard[h, here, :] = probs_b
             centre = jnp.sum(probs * prob_grad, axis=-1, keepdims=True)
             score_grad = (probs * (prob_grad - centre)).astype(BF16)
+            soft[h, here, :] = score_grad
+            attended[here, lanes] = dot(probs_b, v).astype(BF16)
             proj_grad[here, 3 * h * width : (3 * h + 1) * width] = (
                 dot(score_grad, k) * scale
             ).astype(BF16)
-            acc[:, 0:width] += dot(score_grad, q, (0, 0)) * scale
-            acc[:, width : 2 * width] += dot(probs_b, outer, (0, 0))
-            return carry
-
-        lax.fori_loop(0, windows, window, 0)
-        own_grad[h] = acc[0:rows, :]
-        copies = []
-        for side, device in ((0, west), (1, east)):
-            halo_grad_send[side, h] = acc[
-                rows + side * edge : rows + (side + 1) * edge, :
-            ].astype(BF16)
-            copies.append(
-                launch(
-                    remote(
-                        halo_grad_send.at[side, h],
-                        halo_grad.at[side, h],
-                        hgrad_s,
-                        (side, h),
-                        "lon",
-                        device,
+
+    returns = []
+    for first in range(0, heads, 2):
+        some = range(first, min(first + 2, heads))
+        if windows <= 2:
+            for w in range(windows):
+                window(some, w)
+        else:
+            lax.fori_loop(0, windows, lambda w, c, some=some: (window(some, w), c)[1], 0)
+        for h in some:
+            whole = jnp.concatenate(
+                [
+                    dot(soft[h], query[h], (0, 0)),
+                    dot(hard[h], d_out[:, h * width : (h + 1) * width], (0, 0)),
+                ],
+                axis=1,
+            )
+            own_grad[h] = whole[0:rows, :]
+            for side in range(2):
+                halo_grad_send[side, h] = whole[
+                    rows + side * edge : rows + (side + 1) * edge, :
+                ].astype(BF16)
+        for h in some:
+            copies = []
+            for side, device in ((0, west), (1, east)):
+                copies.append(
+                    launch(
+                        remote(
+                            halo_grad_send.at[side, h],
+                            halo_grad.at[side, h],
+                            hgrad_s,
+                            (side, h),
+                            "lon",
+                            device,
+                        )
                     )
                 )
-            )
-        returns.append(copies)
+            returns.append(copies)
 
     sent = []
     for d in range(1, groups):
@@ -234,36 +263,31 @@
             total += dot(pick_ref[side], halo_grad[side, h], (0, 0))
         proj_grad[:, (3 * h + 1) * width : 3 * (h + 1) * width] = total.astype(BF16)
 
-    depth = band.shape[1]
-    half = depth // 2
-    step = min(half, 256)
+    lanes = part.shape[2]
+    lane_blocks = half_in.shape[0]
+    wide = 2 * lanes
 
     def qkv_half(which):
         def one(i, carry):
-            at = pl.multiple_of(which * half + i * step, 128)
-            part[pl.ds(at, step), :] = dot(
-                band[:, pl.ds(at, step)], proj_grad[...], (0, 0)
+            at = which * lane_blocks + 2 * i
+            found = dot(
+                proj_grad[...], band[:, pl.ds(pl.multiple_of(at * lanes, wide), wide)], (0, 0)
             ).astype(BF16)
+            part[at] = found[:, :lanes]
+            part[at + 1] = found[:, lanes:]
             return carry
 
-        lax.fori_loop(0, half // step, one, 0)
+        lax.fori_loop(0, lane_blocks // 2, one, 0)
 
     qkv_half(1 - core)
-    theirs = pl.ds(pl.multiple_of((1 - core) * half, ROW_TILE), half)
-    ours = pl.ds(pl.multiple_of(core * half, ROW_TILE), half)
-    halves = launch(remote(part.at[theirs], half_in, half_s, 0, "lon", pair))
+    halves = launch(
+        remote(part.at[pl.ds((1 - core) * lane_blocks, lane_blocks)], half_in, half_s, 0, "lon", pair)
+    )
     qkv_half(core)
 
-    wide = min(depth, 256)
-
     def latent(i, carry):
-        at = pl.ds(pl.multiple_of(i * wide, 128), wide)
-        total = jnp.zeros((rows, wide), F32)
-        for h in range(heads):
-            total += dot(
-                proj_grad[:, 3 * h * width : 3 * (h + 1) * width], w_ref[h, at, :], (1, 1)
-            )
-        lat_send[:, at] = total.astype(BF16)
+        at = pl.ds(pl.multiple_of(i * wide, wide), wide)
+        lat_send[:, at] = dot(proj_grad[...], w_ref[:, at]).astype(BF16)
         return carry
 
     lax.fori_loop(0, depth // wide, latent, 0)
@@ -277,11 +301,19 @@
     ]
 
     halves.wait_recv()
-    piece = half // chips
-    half_sum[...] = (part[ours, :].astype(F32) + half_in[...].astype(F32)).astype(BF16)
+    ours = pl.ds(core * lane_blocks, lane_blocks)
+    half_sum[...] = (part[ours].astype(F32) + half_in[...].astype(F32)).astype(BF16)
+    piece = chips_in.shape[1]
 
     def piece_of(t):
-        return pl.ds(pl.multiple_of(t * piece, ROW_TILE), piece)
+        return lax.rem(t, lane_blocks), pl.ds(
+            pl.multiple_of(lax.div(t, lane_blocks) * piece, ROW_TILE), piece
+        )
+
+    def result_of(t):
+        lane, here = piece_of(t)
+        at = (core * lane_blocks + lane) * lanes
+        return here, pl.ds(pl.multiple_of(at, lanes), lanes)
 
     exchanged = [
         launch(
@@ -302,19 +334,16 @@
     mixed = jnp.zeros((block, depth), F32)
     for g in range(groups):
         mixed += dot(tokens[g], out_w_ref[g * cols : (g + 1) * cols, :])
-    mixed_ref[...] = mixed.astype(BF16)
+    unpacked(mixed_ref, mixed)
 
     for copy in exchanged:
         copy.wait_recv()
-    total = half_sum[piece_of(chip), :].astype(F32)
+    total = half_sum[piece_of(chip)].astype(F32)
     for d in range(1, chips):
         total += chips_in[d - 1].astype(F32)
 
-    def result_of(t):
-        return pl.ds(pl.multiple_of(core * half + t * piece, ROW_TILE), piece)
-
     final = result_of(chip)
-    qkv_ref[final, :] = total.astype(BF16)
+    qkv_ref[final] = total.astype(BF16)
     spread = [
         launch(
             remote(
@@ -330,7 +359,7 @@
     total = lat_send[mine, :].astype(F32)
     for d in range(1, groups):
         total += lat_in[d - 1].astype(F32)
-    latent_ref[...] = total.astype(BF16)
+    unpacked(latent_ref, total)
 
     for d in range(1, chips):
         spread[d - 1].wait_recv()
@@ -381,13 +410,9 @@
     chips = count // 2
     half = model_width // 2
 
-    def packed(x):
-        x = x.transpose(1, 0, 2, 3).reshape(valid, model_width)
-        return jnp.pad(x, ((0, block - valid), (0, 0)))
-
-    def unpacked(x):
-        return x[:valid].reshape(lat_dev, levels, columns, model_width).transpose(1, 0, 2, 3)
-
+    lanes = 128
+    lane_blocks = half // lanes
+    pieces = max(1, chips // lane_blocks)
     dma = pltpu.SemaphoreType.DMA
     shapes = [
         (groups - 1,),
@@ -405,9 +430,9 @@
     mixed, latent_grad, qkv = pl.pallas_call(
         functools.partial(kernel, (groups, count, heads, width, block, windows, edge)),
         out_shape=(
-            jax.ShapeDtypeStruct((block, model_width), BF16),
-            jax.ShapeDtypeStruct((block, model_width), BF16),
-            jax.ShapeDtypeStruct((model_width, 3 * cols), BF16),
+            jax.ShapeDtypeStruct(latents.shape, BF16),
+            jax.ShapeDtypeStruct(latents.shape, BF16),
+            jax.ShapeDtypeStruct((3 * cols, model_width), BF16),
         ),
         in_specs=[vmem] * 6,
         out_specs=(vmem,) * 3,
@@ -418,17 +443,18 @@
             pltpu.VMEM((heads, rows, width), BF16),
             pltpu.VMEM((heads, keys, 2 * width), BF16),
             pltpu.VMEM((2, heads, edge, 2 * width), BF16),
-            pltpu.VMEM((keys, 2 * width), F32),
+            pltpu.VMEM((heads, rows, keys), BF16),
+            pltpu.VMEM((heads, rows, keys), BF16),
             pltpu.VMEM((2, heads, edge, 2 * width), BF16),
             pltpu.VMEM((2, heads, edge, 2 * width), BF16),
             pltpu.VMEM((heads, rows, 2 * width), F32),
             pltpu.VMEM((rows, cols), BF16),
             pltpu.VMEM((groups, block, cols), BF16),
             pltpu.VMEM((rows, 3 * cols), BF16),
-            pltpu.VMEM((model_width, 3 * cols), BF16),
-            pltpu.VMEM((half, 3 * cols), BF16),
-            pltpu.VMEM((half, 3 * cols), BF16),
-            pltpu.VMEM((chips - 1, half // chips, 3 * cols), BF16),
+            pltpu.VMEM((2 * lane_blocks, 3 * cols, lanes), BF16),
+            pltpu.VMEM((lane_blocks, 3 * cols, lanes), BF16),
+            pltpu.VMEM((lane_blocks, 3 * cols, lanes), BF16),
+            pltpu.VMEM((chips - 1, 3 * cols // pieces, lanes), BF16),
             pltpu.VMEM((rows, model_width), BF16),
             pltpu.VMEM((groups - 1, block, model_width), BF16),
         ]
@@ -437,15 +463,15 @@
             collective_id=0, has_side_effects=True, vmem_limit_bytes=56 * 1024 * 1024
         ),
     )(
-        packed(latents),
-        packed(out_grad),
-        qkv_weight,
+        latents,
+        out_grad,
+        qkv_weight.transpose(0, 2, 1).reshape(3 * cols, model_width),
         out_weight.reshape(-1, model_width),
         jnp.asarray(pick, BF16),
         jnp.asarray(bias),
     )
-    qkv_grad = qkv.reshape(model_width, heads, 3 * width).transpose(1, 0, 2).astype(F32)
-    return unpacked(mixed), unpacked(latent_grad), qkv_grad
+    qkv_grad = qkv.reshape(heads, 3 * width, model_width).transpose(0, 2, 1).astype(F32)
+    return mixed, latent_grad, qkv_grad
 
 
 def solution(mesh):

time: 82.8 us -> 71.6 us (0.86)
  local copies, waits for them, and re-layouts: 12.5 us -> 1.33 us
  other arithmetic: 0 us -> 3.51 us
  Pallas kernels: 69.3 us -> 65.9 us
    convert_element_type x0 -> x1, other arithmetic: none -> 3.51 us  [body(): qkv.reshape(heads, 3 * width, model_width).transpose(0, 2, 1).astype(F32)]
    pallas_call x1, Pallas kernels: 69.3 us -> 65.9 us  [body(): pl.pallas_call(functools.partial(kernel, (groups, count, heads, width, bl...]
    convert_element_type x1 -> x0, local copies, waits for them, and re-layouts: 3.07 us -> none  [body(): qkv.reshape(model_width, heads, 3 * width).transpose(1, 0, 2).astype(F32)]
    transpose x3 -> x0, local copies, waits for them, and re-layouts: 2.57 us -> none  [the longest x2 1.84 us: packed(): x = x.transpose(1, 0, 2, 3).reshape(valid, model_width)]
    unnamed x1 -> x6, local copies, waits for them, and re-layouts: 3.72 us -> 1.33 us
    slice x2 -> x0, local copies, waits for them, and re-layouts: 1.84 us -> none  [unpacked(): x[:valid].reshape(lat_dev, levels, columns, model_width)]
    pad x2 -> x0, local copies, waits for them, and re-layouts: 1.35 us -> none  [packed(): return jnp.pad(x, ((0, block - valid), (0, 0)))]
where the time goes in v2:
time: 71.6 us; the launch traced here: 71.4 us
  Pallas kernels  65.9 us (92%)
  other arithmetic  3.51 us (5%)
  local copies, waits for them, and re-layouts  1.33 us (2%)
    pallas_call x1, Pallas kernels, body(): pl.pallas_call(functools.partial(kernel, (groups, count, heads, width, bl...  65.9 us
    convert_element_type x1, other arithmetic, body(): qkv.reshape(heads, 3 * width, model_width).transpose(0, 2, 1).astype(F32)  3.51 us

profile of v2, /device:TPU:9, one launch (start us, length us, event | category | flops | bytes accessed | tf_op | source)
XLA Modules:
  0.0 71.4 jit_solution(3104503522264248061)
XLA Ops:
  0.6 65.9 %shard_map.85 = (bf16[3,3,8,1024]{3,2,1,0:T(8,128)(2,1)}, bf16[3,3,8,1024]{3,2,1,0:T(8,128)(2,1)}, bf16[768,1024]{1,0:T(8,128)(2,1)}) custom-call(bf16[3,3,8,1024]{3,2,1,0:T(8,128)(2,1)} %lat_ref.1, bf16[3,3,8,1024]{3,2,1,0:T(8,128)(2,1)} %grad_ref.1, bf16[768,1024]{1,0:T(8,128)(2,1)} %bitcast.9, bf16[1024,1024]{1,0:T(8,128)(2,1)} %bitcast.8, ...), custom_call_target="tpu_custom_call" | custom-call | tf_op jit(solution)/shard_map/pallas_call | solution.py:430
  66.6 0.0 copy-start.1
  66.6 0.0 copy-start
  66.6 3.5 %convert_bitcast_fusion = f32[4,1024,192]{1,2,0:T(8,128)} fusion(bf16[4,192,1024]{2,1,0:T(8,128)(2,1)} %bitcast.10), kind=kLoop, calls=%fused_computation | loop fusion | flops 786432 | bytes 4718592 | tf_op jit(solution)/shard_map/convert_element_type | solution.py:473
  70.1 0.0 copy-done.1
  70.1 0.7 copy.11
  70.7 0.0 copy-done
  70.8 0.7 copy.12
Async XLA Ops:
  66.6 3.5 %copy-start.1 = (bf16[3,3,8,1024]{3,2,1,0:T(8,128)(2,1)S(1)}, bf16[3,3,8,1024]{3,2,1,0:T(8,128)(2,1)}, u32[]{:S(2)}) copy-start(bf16[3,3,8,1024]{3,2,1,0:T(8,128)(2,1)} %get-tuple-element.12) | copy-start | bytes 442372
  66.6 4.2 %copy-start = (bf16[3,3,8,1024]{3,2,1,0:T(8,128)(2,1)S(1)}, bf16[3,3,8,1024]{3,2,1,0:T(8,128)(2,1)}, u32[]{:S(2)}) copy-start(bf16[3,3,8,1024]{3,2,1,0:T(8,128)(2,1)} %get-tuple-element.13) | copy-start | bytes 442372

commit v3 on v2

--- a/solution.py
+++ b/solution.py
@@ -39,13 +39,15 @@
     dims,
     lat_ref,
     grad_ref,
-    w_ref,
-    out_w_ref,
+    w_in,
+    out_w_in,
     pick_ref,
     bias_ref,
     mixed_ref,
     latent_ref,
     qkv_ref,
+    w_ref,
+    out_w_ref,
     band,
     d_out,
     grad_send,
@@ -96,6 +98,10 @@
     def block_of(g):
         return pl.ds(pl.multiple_of(g * block, ROW_TILE), block)
 
+    out_w_load = pltpu.make_async_copy(out_w_in, out_w_ref, sems[20].at[0])
+    out_w_load.start()
+    w_load = pltpu.make_async_copy(w_in, w_ref, sems[20].at[1])
+    w_load.start()
     mine = block_of(row)
     def packed(ref):
         parts = [ref[level, r].astype(F32) for r in range(lat_dev) for level in range(levels)]
@@ -135,6 +141,7 @@
         for d in range(1, groups)
     ]
     out_grad = packed(grad_ref)
+    out_w_load.wait()
     grads = []
     for d in range(1, groups + 1):
         g = partner(d)
@@ -152,6 +159,7 @@
         copy.wait_recv()
 
     halos = []
+    w_load.wait()
     projected = dot(band[...], w_ref[...], (1, 1)).astype(BF16)
     for h in range(heads):
         base = 3 * h * width
@@ -434,9 +442,11 @@
             jax.ShapeDtypeStruct(latents.shape, BF16),
             jax.ShapeDtypeStruct((3 * cols, model_width), BF16),
         ),
-        in_specs=[vmem] * 6,
+        in_specs=[vmem] * 2 + [pl.BlockSpec(memory_space=pl.ANY)] * 2 + [vmem] * 2,
         out_specs=(vmem,) * 3,
         scratch_shapes=[
+            pltpu.VMEM((3 * cols, model_width), BF16),
+            pltpu.VMEM((groups * cols, model_width), BF16),
             pltpu.VMEM((rows, model_width), BF16),
             pltpu.VMEM((rows, cols), BF16),
             pltpu.VMEM((groups - 1, block, cols), BF16),
@@ -458,7 +468,8 @@
             pltpu.VMEM((rows, model_width), BF16),
             pltpu.VMEM((groups - 1, block, model_width), BF16),
         ]
-        + [dma(s) for s in shapes for _ in range(2)],
+        + [dma(s) for s in shapes for _ in range(2)]
+        + [dma((2,))],
         compiler_params=pltpu.CompilerParams(
             collective_id=0, has_side_effects=True, vmem_limit_bytes=56 * 1024 * 1024
         ),

time: 71.6 us -> 70.5 us (0.985)
  Pallas kernels: 65.9 us -> 64.9 us
    pallas_call x1, Pallas kernels: 65.9 us -> 64.9 us  [body(): pl.pallas_call(functools.partial(kernel, (groups, count, heads, width, bl...]
where the time goes in v3:
time: 70.5 us; the launch traced here: 70.4 us
  Pallas kernels  64.9 us (92%)
  other arithmetic  3.51 us (5%)
  local copies, waits for them, and re-layouts  1.33 us (2%)
    pallas_call x1, Pallas kernels, body(): pl.pallas_call(functools.partial(kernel, (groups, count, heads, width, bl...  64.9 us
    convert_element_type x1, other arithmetic, body(): qkv.reshape(heads, 3 * width, model_width).transpose(0, 2, 1).astype(F32)  3.51 us

profile of v3, /device:TPU:9, one launch (start us, length us, event | category | flops | bytes accessed | tf_op | source)
XLA Modules:
  0.0 70.4 jit_solution(627449964331591840)
XLA Ops:
  0.6 64.9 %shard_map.85 = (bf16[3,3,8,1024]{3,2,1,0:T(8,128)(2,1)}, bf16[3,3,8,1024]{3,2,1,0:T(8,128)(2,1)}, bf16[768,1024]{1,0:T(8,128)(2,1)}) custom-call(bf16[3,3,8,1024]{3,2,1,0:T(8,128)(2,1)} %lat_ref.1, bf16[3,3,8,1024]{3,2,1,0:T(8,128)(2,1)} %grad_ref.1, bf16[768,1024]{1,0:T(8,128)(2,1)} %bitcast.9, bf16[1024,1024]{1,0:T(8,128)(2,1)} %bitcast.8, ...), custom_call_target="tpu_custom_call" | custom-call | tf_op jit(solution)/shard_map/pallas_call | solution.py:438
  65.5 0.0 copy-start.1
  65.5 0.0 copy-start
  65.5 3.5 %convert_bitcast_fusion = f32[4,1024,192]{1,2,0:T(8,128)} fusion(bf16[4,192,1024]{2,1,0:T(8,128)(2,1)} %bitcast.10), kind=kLoop, calls=%fused_computation | loop fusion | flops 786432 | bytes 4718592 | tf_op jit(solution)/shard_map/convert_element_type | solution.py:484
  69.0 0.0 copy-done.1
  69.0 0.7 copy.11
  69.7 0.0 copy-done
  69.7 0.7 copy.12
Async XLA Ops:
  65.5 3.5 %copy-start.1 = (bf16[3,3,8,1024]{3,2,1,0:T(8,128)(2,1)S(1)}, bf16[3,3,8,1024]{3,2,1,0:T(8,128)(2,1)}, u32[]{:S(2)}) copy-start(bf16[3,3,8,1024]{3,2,1,0:T(8,128)(2,1)} %get-tuple-element.12) | copy-start | bytes 442372
  65.5 4.2 %copy-start = (bf16[3,3,8,1024]{3,2,1,0:T(8,128)(2,1)S(1)}, bf16[3,3,8,1024]{3,2,1,0:T(8,128)(2,1)}, u32[]{:S(2)}) copy-start(bf16[3,3,8,1024]{3,2,1,0:T(8,128)(2,1)} %get-tuple-element.13) | copy-start | bytes 442372
